TPU v7x, 32 devices: a whole 2x2x4 slice. The times are simulated.
32 devices in a mesh: ctx: 8 (over z, x), grp: 4 (over y, core).
Axes of the slice: x: 2, y: 2, z: 4, core: 2. Of those that a mesh axis runs over, the one named last changes fastest.
Arguments:
- query: bfloat16 [128, 2560], P('ctx', 'grp'), may hold values from -8 to 8
- keys: bfloat16 [32768, 512], P('ctx', 'grp'), may hold values from -16 to 16
- values: bfloat16 [32768, 512], P('ctx', 'grp'), may hold values from -6 to 6
- blocks: int32 [128, 8, 8], P(None, 'ctx'), may hold values from 0 to 31, as said below
Outputs:
- attended: bfloat16 [128, 2560], P(('ctx', 'grp'))
Inputs may be any that keep to these rules, and one draw needn't show every extreme that they name: Each row's list for each context shard names 8 different blocks, the first of them block 0.
All inputs are finite; a program needn't handle non-finite values.
Results may differ from a plain program's by a relative error of at most 0.012.
Values may be sent and summed in bfloat16 or wider, within the bound.
A program may use at most 192 MiB of HBM per device.

v0:
```python
import math

import jax
import jax.numpy as jnp
from jax import lax
from jax.sharding import PartitionSpec as P

HD = 128
QPK = 5
BLOCK = 128


def per_device(query, keys, values, blocks):
    whole = lax.all_gather(query, "ctx", axis=0, tiled=True)
    row_count = whole.shape[0]
    ctx_dev = keys.shape[0]
    score_scale = 1.0 / math.sqrt(HD)
    listed_here = blocks[:, 0, :]
    block_count = ctx_dev // BLOCK
    block_ids = jnp.arange(block_count, dtype=jnp.int32)
    listed_hits = jnp.any(listed_here[:, :, None] == block_ids[None, None, :], axis=1)
    key_span = min(512, ctx_dev)
    turn_count = ctx_dev // key_span
    span_blocks = key_span // BLOCK
    query_group = whole.reshape(row_count * QPK, HD)

    def scores_at(block_index):
        key_block = lax.dynamic_slice_in_dim(keys, block_index * key_span, key_span, 0)
        scores = jnp.einsum("id,td->it", query_group, key_block, preferred_element_type=jnp.float32)
        scores = scores.reshape(row_count, QPK, key_span) * score_scale
        block_hits = lax.dynamic_slice_in_dim(
            listed_hits, block_index * span_blocks, span_blocks, 1
        )
        block_mask = jnp.repeat(block_hits, BLOCK, axis=1)[:, None, :]
        return (scores, block_mask)

    def first_pass(block_index, running_max):
        scores, block_mask = scores_at(block_index)
        return jnp.maximum(running_max, jnp.max(jnp.where(block_mask, scores, -jnp.inf), axis=-1))

    local_max = lax.fori_loop(
        0, turn_count, first_pass, jnp.full((row_count, QPK), -jnp.inf, jnp.float32)
    )

    def second_pass(block_index, carry):
        denominator, numerator = carry
        scores, block_mask = scores_at(block_index)
        weights = jnp.where(block_mask, jnp.exp(scores - local_max[..., None]), 0.0)
        denominator = denominator + jnp.sum(weights, axis=-1)
        rounded = weights.astype(jnp.bfloat16).reshape(row_count * QPK, key_span)
        value_block = lax.dynamic_slice_in_dim(values, block_index * key_span, key_span, 0)
        numerator = numerator + jnp.dot(rounded, value_block, preferred_element_type=jnp.float32)
        return (denominator, numerator)

    start_carry = (
        jnp.zeros((row_count, QPK), jnp.float32),
        jnp.zeros((row_count * QPK, HD), jnp.float32),
    )
    local_sum, local_out = lax.fori_loop(0, turn_count, second_pass, start_carry)
    out_parts = local_out.reshape(row_count, QPK * HD)
    part_out = (out_parts / jnp.repeat(local_sum, HD, axis=1)).astype(jnp.bfloat16)
    log_total = local_max + jnp.log(local_sum)
    global_top = lax.pmax(log_total, "ctx")
    factor = jnp.exp(log_total - global_top)
    scaled_out = part_out.astype(jnp.float32) * jnp.repeat(factor, HD, axis=1)
    numerator, denominator = (
        lax.psum_scatter(scaled_out, "ctx", scatter_dimension=0, tiled=True),
        lax.psum_scatter(factor, "ctx", scatter_dimension=0, tiled=True),
    )
    finished = (numerator / jnp.repeat(denominator, HD, axis=1)).astype(jnp.bfloat16)
    return lax.all_to_all(finished, "grp", split_axis=0, concat_axis=1, tiled=True)


def solution(mesh):
    placed = (P("ctx", "grp"), P("ctx", "grp"), P("ctx", "grp"), P(None, "ctx", None))
    return jax.shard_map(
        per_device, mesh=mesh, in_specs=placed, out_specs=P(("ctx", "grp"), None), check_vma=False
    )
```

profile of v0, /device:TPU:0, one launch (start us, length us, event | category | flops | bytes accessed | tf_op | source)
XLA Modules:
  0.0 275.5 jit_solution(5922573177241698614)
XLA Ops:
  7.4 32.6 %all_gather.3 = bf16[128,640]{1,0:T(8,128)(2,1)S(1)} all-gather(bf16[16,640]{1,0:T(8,128)(2,1)} %param.8), channel_id=1, replica_groups=mesh['ctx'=8,'grp'=4] {'ctx'}, dimensions={0}, use_global_device_ids=true | all-gather | bytes 184320 | tf_op jit(solution)/shard_map/all_gather | solution.py:14
  40.1 23.0 %while.31 = (s32[]{:T(128)}, f32[128,5]{1,0:T(8,128)S(1)}, pred[128,32]{1,0:T(8,128)(4,1)S(1)}, bf16[4096,128]{1,0:T(8,128)(2,1)}, bf16[640,128]{1,0:T(8,128)(2,...) while((s32[]{:T(128)}, f32[128,5]{1,0:T(8,128)S(1)}, ...), condition=%wide.region_3.4_spmd.clone, body=%wide.region_1.3_spmd.clone.sunk | while | flops 84869768 | bytes 2540259 | solution.py:41
  41.4 1.3 fusion.33
  63.8 35.0 %while.32 = (s32[]{:T(128)}, f32[128,5]{1,0:T(8,128)S(1)}, f32[640,128]{1,0:T(8,128)S(1)}, pred[128,32]{1,0:T(8,128)(4,1)S(1)}, bf16[4096,128]{1,0:T(8,128)(2,1)...) while((s32[]{:T(128)}, f32[128,5]{1,0:T(8,128)S(1)}, ...), condition=%wide.wide.region_6.7_spmd.clone, body=%wide.wide.region_4.6_spmd.clone.sunk | while | flops 169575040 | bytes 4640008 | solution.py:59
  65.1 1.4 fusion.37
  66.8 1.3 convolution_add_fusion.3
  69.5 1.4 fusion.37
  71.1 1.3 convolution_add_fusion.3
  73.8 1.4 fusion.37
  75.5 1.3 convolution_add_fusion.3
  78.2 1.4 fusion.37
  79.9 1.3 convolution_add_fusion.3
  82.6 1.4 fusion.37
  84.3 1.3 convolution_add_fusion.3
  87.0 1.4 fusion.37
  88.7 1.3 convolution_add_fusion.3
  91.4 1.4 fusion.37
  93.0 1.3 convolution_add_fusion.3
  95.7 1.4 fusion.37
  97.4 1.3 convolution_add_fusion.3
  99.6 37.4 %pmax.7 = f32[128,5]{1,0:T(8,128)S(1)} all-reduce(f32[128,5]{1,0:T(8,128)S(1)} %log_add_fusion), channel_id=1, replica_groups=mesh['ctx'=8,'grp'=4] {'ctx'}, use_global_device_ids=true, to_apply=%region_7.8 | all-reduce | flops 640 | bytes 5120 | tf_op jit(solution)/shard_map/pmax | solution.py:63
  140.0 56.4 %reduce-scatter.5.cloned.1.call-done = f32[16,5]{1,0:T(8,128)} async-done(((f32[128,5]{1,0:T(8,128)}), f32[16,5]{1,0:T(8,128)}) %reduce-scatter.5.cloned.1.call-update) | async-done | bytes 336 | tf_op jit(solution)/shard_map/reduce_scatter | solution.py:68
  196.4 63.6 %reduce-scatter.3.cloned.1.call-done = f32[16,640]{1,0:T(8,128)} async-done(((f32[128,640]{1,0:T(8,128)}), f32[16,640]{1,0:T(8,128)}) %reduce-scatter.3.cloned.1.call-update) | async-done | bytes 40976 | tf_op jit(solution)/shard_map/reduce_scatter | solution.py:67
  261.6 6.4 %all_to_all.19 = bf16[4,4,640]{2,1,0:T(4,128)(2,1)S(1)} all-to-all(bf16[4,4,640]{2,1,0:T(4,128)(2,1)S(1)} %all_to_all.14), channel_id=1, replica_groups=mesh['ctx'=8,'grp'=4] {'grp'}, dimensions={0} | all-to-all | bytes 40960 | tf_op jit(solution)/shard_map/all_to_all | solution.py:71
  (162 shorter events, 40.6 us)
Async XLA Ops:
  6.5 189.9 %reduce-scatter.5.cloned.1.call-start = ((), (), s32[]{:S(2)}) async-start(), calls=%async_computation.4 | async-start | bytes 73728 | tf_op jit(solution)/shard_map/reduce_scatter | solution.py:68
  63.1 0.6 copy-start
  137.7 122.3 %reduce-scatter.3.cloned.1.call-start = ((), (), s32[]{:S(2)}) async-start(), calls=%async_computation.3 | async-start | bytes 368640 | tf_op jit(solution)/shard_map/reduce_scatter | solution.py:67
Sparse Core Ops, SparseCore 0:
  137.8 58.5 reduce-scatter.4
  199.7 60.2 reduce-scatter.2
where the time goes:
time: 276 us; the launch traced here: 275 us
  waiting for transfers between devices  120 us (43%)
  blocking collectives  76.4 us (28%)
  matrix products  32.6 us (12%)
  local copies, waits for them, and re-layouts  27.4 us (10%)
  between operations  13.5 us (5%)
  other arithmetic  4.08 us (1%)
    reduce_scatter x1, waiting for transfers between devices, per_device(): lax.psum_scatter(scaled_out, 'ctx', scatter_dimension=0, tiled=True)  63.6 us
    reduce_scatter x1, waiting for transfers between devices, per_device(): lax.psum_scatter(factor, 'ctx', scatter_dimension=0, tiled=True)  56.4 us
    pmax x1, blocking collectives, per_device(): global_top = lax.pmax(log_total, 'ctx')  37.4 us
    all_gather x1, blocking collectives, per_device(): whole = lax.all_gather(query, 'ctx', axis=0, tiled=True)  32.6 us
    dot_general x16, matrix products, scores_at(): jnp.einsum('id,td->it', query_group, key_block, preferred_element_type=jn...  21.9 us
    dot_general x8, matrix products, second_pass(): jnp.dot(rounded, value_block, preferred_element_type=jnp.float32)  10.7 us
    broadcast_in_dim x24, local copies, waits for them, and re-layouts, second_pass(): weights = jnp.where(block_mask, jnp.exp(scores - local_max[..., None]), 0.0)  7.75 us
    broadcast_in_dim x24, local copies, waits for them, and re-layouts, first_pass(): jnp.where(block_mask, scores, -jnp.inf)  7.75 us
  transfers between devices with their start and end apart: 2, of which 2 were waited for; matrix products, arithmetic and copies ran while one was open for 1% of the time, Pallas kernels for 0%

commit v1 on v0

v1 whole, which is shorter than its diff:
```python
import functools
import math

import jax
import jax.numpy as jnp
from jax import lax
from jax.experimental import pallas as pl
from jax.experimental.pallas import tpu as pltpu
from jax.sharding import PartitionSpec as P

HD = 128
QPK = 5
BLOCK = 128
LANES = 128
NEG = -1e30
PAD = 16
SLOTS_PER_TURN = 2
CHUNK = 1024
MESH = pl.DeviceIdType.MESH


def xor(a, b, n):
    total, bit = 0, 1
    while bit < n:
        total = total + bit * ((a // bit + b // bit) % 2)
        bit *= 2
    return total


def kernel(
    n, ng, q_ref, k_ref, v_ref, b_ref, o_ref,
    qbuf, kext, vext, mask, score, part_out, part_in, fin_out, fin_in,
    local_sem, qsend, qrecv, psend, precv, fsend, frecv,
):
    me = lax.axis_index("ctx")
    grp = lax.axis_index("grp")
    own_rows = qbuf.shape[1]
    group_rows = QPK * own_rows
    tokens = kext.shape[0]
    row_count = mask.shape[0]
    log2_scale = math.log2(math.e) / math.sqrt(HD)

    barrier = pltpu.get_barrier_semaphore()
    for k in range(1, n):
        pl.semaphore_signal(barrier, inc=1, device_id={"ctx": xor(me, k, n)}, device_id_type=MESH)
    for j in range(1, ng):
        pl.semaphore_signal(barrier, inc=1, device_id={"grp": xor(grp, j, ng)}, device_id_type=MESH)

    load_q = pltpu.make_async_copy(q_ref, qbuf.at[0], local_sem.at[0])
    load_k = pltpu.make_async_copy(k_ref, kext.at[:, 0:HD], local_sem.at[1])
    load_v = pltpu.make_async_copy(v_ref, vext.at[:, 0:HD], local_sem.at[2])
    load_q.start()
    load_k.start()
    load_v.start()

    def query_copy(k):
        return pltpu.make_async_remote_copy(
            src_ref=qbuf.at[0], dst_ref=qbuf.at[k], send_sem=qsend.at[k], recv_sem=qrecv.at[k],
            device_id={"ctx": xor(me, k, n)}, device_id_type=MESH,
        )

    def part_copy(k):
        return pltpu.make_async_remote_copy(
            src_ref=part_out.at[k], dst_ref=part_in.at[k], send_sem=psend.at[k], recv_sem=precv.at[k],
            device_id={"ctx": xor(me, k, n)}, device_id_type=MESH,
        )

    def fin_copy(j):
        return pltpu.make_async_remote_copy(
            src_ref=fin_out, dst_ref=fin_in.at[j], send_sem=fsend.at[j], recv_sem=frecv.at[j],
            device_id={"grp": xor(grp, j, ng)}, device_id_type=MESH,
        )

    pl.semaphore_wait(barrier, n - 1 + ng - 1)
    load_q.wait()
    for k in range(1, n):
        query_copy(k).start()

    lane = lax.broadcasted_iota(jnp.int32, (BLOCK, LANES), 1)
    for b in range(tokens // BLOCK):
        kext[b * BLOCK:(b + 1) * BLOCK, HD:] = jnp.where(lane == b, 1.0, 0.0).astype(jnp.bfloat16)
    vext[:, HD:] = jnp.ones((tokens, LANES), jnp.bfloat16)
    listed = b_ref[...]
    block_row = lax.broadcasted_iota(jnp.int32, (tokens // BLOCK, row_count), 0)
    hit = block_row == listed[0:1, :]
    for i in range(1, listed.shape[0]):
        hit = hit | (block_row == listed[i:i + 1, :])
    bias = jnp.where(hit, 0.0, NEG)
    unused = jnp.zeros((LANES - tokens // BLOCK, row_count), jnp.float32)
    mask[...] = jnp.transpose(jnp.concatenate([bias, unused], axis=0)).astype(jnp.bfloat16)

    diag = (
        lax.broadcasted_iota(jnp.int32, (group_rows, LANES), 0)
        == lax.broadcasted_iota(jnp.int32, (group_rows, LANES), 1)
    )
    pad_row = lax.broadcasted_iota(jnp.int32, (PAD, LANES), 0)
    load_k.wait()
    load_v.wait()

    def turn(t, carry):
        pieces = []
        for u in range(SLOTS_PER_TURN):
            k = t * SLOTS_PER_TURN + u

            @pl.when(k > 0)
            def _():
                query_copy(k).wait_recv()

            owner = xor(me, k, n)
            bias = mask[pl.ds(pl.multiple_of(owner * own_rows, own_rows), own_rows), :]
            rows = qbuf[k]
            for h in range(QPK):
                pieces.append(jnp.concatenate([rows[:, h * HD:(h + 1) * HD], bias], axis=1))
        query = jnp.concatenate(pieces, axis=0)
        top = None
        for c in range(0, tokens, CHUNK):
            s = lax.dot_general(
                query, kext[c:c + CHUNK, :], (((1,), (1,)), ((), ())), preferred_element_type=jnp.float32
            )
            score[:, c:c + CHUNK] = s
            for i in range(0, CHUNK, LANES):
                part = s[:, i:i + LANES]
                top = part if top is None else jnp.maximum(top, part)
        top = jnp.max(top, axis=1, keepdims=True)
        total = None
        for c in range(0, tokens, CHUNK):
            w = jnp.exp2((score[:, c:c + CHUNK] - top) * log2_scale).astype(jnp.bfloat16)
            piece = jnp.dot(w, vext[c:c + CHUNK, :], preferred_element_type=jnp.float32)
            total = piece if total is None else total + piece
        weight = total[:, HD:]
        part = (total[:, :HD] / weight).astype(jnp.bfloat16)
        lse = top * (1.0 / math.sqrt(HD)) + jnp.log(weight)
        for u in range(SLOTS_PER_TURN):
            k = t * SLOTS_PER_TURN + u
            at = slice(u * group_rows, (u + 1) * group_rows)
            line = jnp.sum(jnp.where(diag, lse[at], 0.0), axis=0, keepdims=True)
            high = line.astype(jnp.bfloat16).astype(jnp.float32)
            mid = (line - high).astype(jnp.bfloat16).astype(jnp.float32)
            low = line - high - mid
            tail = jnp.where(pad_row == 0, high, jnp.where(pad_row == 1, mid, jnp.where(pad_row == 2, low, 0.0)))
            part_out[k, 0:group_rows, :] = part[at]
            part_out[k, group_rows:, :] = tail.astype(jnp.bfloat16)

            @pl.when(k > 0)
            def _():
                part_copy(k).start()

        return carry

    lax.fori_loop(0, n // SLOTS_PER_TURN, turn, 0)

    for k in range(1, n):
        part_copy(k).wait_recv()
    parts = [part_out.at[0]] + [part_in.at[k] for k in range(1, n)]
    lines = [jnp.sum(p[group_rows:, :].astype(jnp.float32), axis=0, keepdims=True) for p in parts]
    best = functools.reduce(jnp.maximum, lines)
    factors = [jnp.exp(x - best) for x in lines]
    denominator = sum(factors[1:], factors[0])
    factors.append(jnp.zeros((LANES - n, LANES), jnp.float32))
    columns = jnp.transpose(jnp.concatenate(factors, axis=0) / denominator)
    result = None
    for k, p in enumerate(parts):
        piece = p[0:group_rows, :].astype(jnp.float32) * columns[0:group_rows, k:k + 1]
        result = piece if result is None else result + piece
    for h in range(QPK):
        fin_out[:, h * HD:(h + 1) * HD] = result[h * own_rows:(h + 1) * own_rows].astype(jnp.bfloat16)
    for j in range(1, ng):
        fin_copy(j).start()

    out_rows = own_rows // ng
    width = QPK * HD
    for j in range(ng):
        if j > 0:
            fin_copy(j).wait_recv()
        whole = (fin_out if j == 0 else fin_in.at[j])[...].astype(jnp.float32)
        mine = whole[0:out_rows]
        for g in range(1, ng):
            mine = jnp.where(grp == g, whole[g * out_rows:(g + 1) * out_rows], mine)
        origin = xor(grp, j, ng)
        o_ref[:, pl.ds(pl.multiple_of(origin * width, LANES), width)] = mine.astype(jnp.bfloat16)

    for k in range(1, n):
        query_copy(k).wait_send()
        part_copy(k).wait_send()
    for j in range(1, ng):
        fin_copy(j).wait_send()


def per_device(n, ng, query, keys, values, blocks):
    own_rows, width = query.shape
    tokens = keys.shape[0]
    rows = blocks.shape[0]
    message = QPK * own_rows + PAD
    any_spec = pl.BlockSpec(memory_space=pl.ANY)
    vmem_spec = pl.BlockSpec(memory_space=pltpu.VMEM)
    return pl.pallas_call(
        functools.partial(kernel, n, ng),
        out_shape=jax.ShapeDtypeStruct((own_rows // ng, width * ng), jnp.bfloat16),
        in_specs=[any_spec, any_spec, any_spec, vmem_spec],
        out_specs=vmem_spec,
        scratch_shapes=[
            pltpu.VMEM((n, own_rows, width), jnp.bfloat16),
            pltpu.VMEM((tokens, 2 * HD), jnp.bfloat16),
            pltpu.VMEM((tokens, 2 * HD), jnp.bfloat16),
            pltpu.VMEM((rows, LANES), jnp.bfloat16),
            pltpu.VMEM((SLOTS_PER_TURN * QPK * own_rows, tokens), jnp.float32),
            pltpu.VMEM((n, message, HD), jnp.bfloat16),
            pltpu.VMEM((n, message, HD), jnp.bfloat16),
            pltpu.VMEM((own_rows, width), jnp.bfloat16),
            pltpu.VMEM((ng, own_rows, width), jnp.bfloat16),
            pltpu.SemaphoreType.DMA((3,)),
            pltpu.SemaphoreType.DMA((n,)),
            pltpu.SemaphoreType.DMA((n,)),
            pltpu.SemaphoreType.DMA((n,)),
            pltpu.SemaphoreType.DMA((n,)),
            pltpu.SemaphoreType.DMA((ng,)),
            pltpu.SemaphoreType.DMA((ng,)),
        ],
        compiler_params=pltpu.CompilerParams(
            collective_id=0, has_side_effects=True, vmem_limit_bytes=60 * 1024 * 1024
        ),
    )(query, keys, values, jnp.transpose(blocks, (1, 2, 0))[0])


def solution(mesh):
    placed = (P("ctx", "grp"), P("ctx", "grp"), P("ctx", "grp"), P(None, "ctx", None))
    body = functools.partial(per_device, mesh.shape["ctx"], mesh.shape["grp"])
    return jax.shard_map(
        body, mesh=mesh, in_specs=placed, out_specs=P(("ctx", "grp"), None), check_vma=False
    )
```

time: 276 us -> 27 us (0.10)
  waiting for transfers between devices: 120 us -> 0 us
  blocking collectives: 76.4 us -> 0 us
  matrix products: 32.6 us -> 0 us
  local copies, waits for them, and re-layouts: 27.4 us -> 1.34 us
  Pallas kernels: 0 us -> 25.5 us
  between operations: 13.5 us -> 0.01 us
  other arithmetic: 4.08 us -> 0 us
    reduce_scatter x2 -> x0, waiting for transfers between devices: 120 us -> none  [the longest x1 63.6 us: per_device(): lax.psum_scatter(scaled_out, 'ctx', scatter_dimension=0, tiled=True)]
    pmax x1 -> x0, blocking collectives: 37.4 us -> none  [per_device(): global_top = lax.pmax(log_total, 'ctx')]
    dot_general x24 -> x0, matrix products: 32.6 us -> none  [the longest x16 21.9 us: scores_at(): jnp.einsum('id,td->it', query_group, key_block, preferred_element_type=jn...]
    all_gather x1 -> x0, blocking collectives: 32.6 us -> none  [per_device(): whole = lax.all_gather(query, 'ctx', axis=0, tiled=True)]
    pallas_call x0 -> x1, Pallas kernels: none -> 25.5 us  [per_device(): pl.pallas_call(functools.partial(kernel, n, ng), out_shape=jax.ShapeDtype...]
    broadcast_in_dim x67 -> x0, local copies, waits for them, and re-layouts: 19.5 us -> none  [the longest x24 7.75 us: second_pass(): weights = jnp.where(block_mask, jnp.exp(scores - local_max[..., None]), 0.0)]
    all_to_all x1 -> x0, blocking collectives: 6.41 us -> none  [per_device(): lax.all_to_all(finished, 'grp', split_axis=0, concat_axis=1, tiled=True)]
  transfers between devices with their start and end apart: 2 -> 0, of which waited for: 2 -> 0; matrix products, arithmetic and copies ran while one was open for 1% -> 0% of each run, Pallas kernels for 0% -> 0%
where the time goes in v1:
time: 27 us; the launch traced here: 26.8 us
  Pallas kernels  25.5 us (94%)
  local copies, waits for them, and re-layouts  1.34 us (5%)
    pallas_call x1, Pallas kernels, per_device(): pl.pallas_call(functools.partial(kernel, n, ng), out_shape=jax.ShapeDtype...  25.5 us
    unnamed x1, local copies, waits for them, and re-layouts  1.34 us

profile of v1, /device:TPU:0, one launch (start us, length us, event | category | flops | bytes accessed | tf_op | source)
XLA Modules:
  0.0 26.8 jit_solution(3503823474108979762)
XLA Ops:
  0.0 25.5 %shard_map.46 = bf16[4,2560]{1,0:T(4,128)(2,1)} custom-call(bf16[16,640]{1,0:T(8,128)(2,1)} %q_ref.1, bf16[4096,128]{1,0:T(8,128)(2,1)} %k_ref.1, bf16[4096,128]{1,0:T(8,128)(2,1)} %v_ref.1, s32[8,128]{1,0:T(8,128)} %bitcast.3), custom_call_target="tpu_custom_call" | custom-call | tf_op jit(solution)/shard_map/pallas_call | solution.py:196
  25.5 1.3 %copy.6 = bf16[4,2560]{1,0:T(4,128)(2,1)} copy(bf16[4,2560]{1,0:T(4,128)(2,1)} %shard_map.46) | data formatting | bytes 40960

commit v2 on v1

--- a/solution.py
+++ b/solution.py
@@ -29,16 +29,16 @@
 
 def kernel(
     n, ng, q_ref, k_ref, v_ref, b_ref, o_ref,
-    qbuf, kext, vext, mask, score, part_out, part_in, fin_out, fin_in,
+    qbuf, kbuf, kext, vext, mask, score, part_out, part_in, fin_out, fin_in,
     local_sem, qsend, qrecv, psend, precv, fsend, frecv,
 ):
     me = lax.axis_index("ctx")
     grp = lax.axis_index("grp")
     own_rows = qbuf.shape[1]
     group_rows = QPK * own_rows
-    tokens = kext.shape[0]
+    tokens = kbuf.shape[0]
     row_count = mask.shape[0]
-    log2_scale = math.log2(math.e) / math.sqrt(HD)
+    scale = 1.0 / math.sqrt(HD)
 
     barrier = pltpu.get_barrier_semaphore()
     for k in range(1, n):
@@ -47,7 +47,7 @@
         pl.semaphore_signal(barrier, inc=1, device_id={"grp": xor(grp, j, ng)}, device_id_type=MESH)
 
     load_q = pltpu.make_async_copy(q_ref, qbuf.at[0], local_sem.at[0])
-    load_k = pltpu.make_async_copy(k_ref, kext.at[:, 0:HD], local_sem.at[1])
+    load_k = pltpu.make_async_copy(k_ref, kbuf, local_sem.at[1])
     load_v = pltpu.make_async_copy(v_ref, vext.at[:, 0:HD], local_sem.at[2])
     load_q.start()
     load_k.start()
@@ -76,9 +76,9 @@
     for k in range(1, n):
         query_copy(k).start()
 
-    lane = lax.broadcasted_iota(jnp.int32, (BLOCK, LANES), 1)
+    sub = lax.broadcasted_iota(jnp.int32, (LANES, BLOCK), 0)
     for b in range(tokens // BLOCK):
-        kext[b * BLOCK:(b + 1) * BLOCK, HD:] = jnp.where(lane == b, 1.0, 0.0).astype(jnp.bfloat16)
+        kext[HD:, b * BLOCK:(b + 1) * BLOCK] = jnp.where(sub == b, 1.0, 0.0).astype(jnp.bfloat16)
     vext[:, HD:] = jnp.ones((tokens, LANES), jnp.bfloat16)
     listed = b_ref[...]
     block_row = lax.broadcasted_iota(jnp.int32, (tokens // BLOCK, row_count), 0)
@@ -95,6 +95,9 @@
     )
     pad_row = lax.broadcasted_iota(jnp.int32, (PAD, LANES), 0)
     load_k.wait()
+    for b in range(tokens // BLOCK):
+        at = slice(b * BLOCK, (b + 1) * BLOCK)
+        kext[0:HD, at] = jnp.transpose(kbuf[at, :].astype(jnp.float32)).astype(jnp.bfloat16)
     load_v.wait()
 
     def turn(t, carry):
@@ -114,9 +117,7 @@
         query = jnp.concatenate(pieces, axis=0)
         top = None
         for c in range(0, tokens, CHUNK):
-            s = lax.dot_general(
-                query, kext[c:c + CHUNK, :], (((1,), (1,)), ((), ())), preferred_element_type=jnp.float32
-            )
+            s = jnp.dot(query, kext[:, c:c + CHUNK], preferred_element_type=jnp.float32)
             score[:, c:c + CHUNK] = s
             for i in range(0, CHUNK, LANES):
                 part = s[:, i:i + LANES]
@@ -124,12 +125,12 @@
         top = jnp.max(top, axis=1, keepdims=True)
         total = None
         for c in range(0, tokens, CHUNK):
-            w = jnp.exp2((score[:, c:c + CHUNK] - top) * log2_scale).astype(jnp.bfloat16)
+            w = jnp.exp((score[:, c:c + CHUNK] - top) * scale).astype(jnp.bfloat16)
             piece = jnp.dot(w, vext[c:c + CHUNK, :], preferred_element_type=jnp.float32)
             total = piece if total is None else total + piece
         weight = total[:, HD:]
         part = (total[:, :HD] / weight).astype(jnp.bfloat16)
-        lse = top * (1.0 / math.sqrt(HD)) + jnp.log(weight)
+        lse = top * scale + jnp.log(weight)
         for u in range(SLOTS_PER_TURN):
             k = t * SLOTS_PER_TURN + u
             at = slice(u * group_rows, (u + 1) * group_rows)
@@ -200,7 +201,8 @@
         out_specs=vmem_spec,
         scratch_shapes=[
             pltpu.VMEM((n, own_rows, width), jnp.bfloat16),
-            pltpu.VMEM((tokens, 2 * HD), jnp.bfloat16),
+            pltpu.VMEM((tokens, HD), jnp.bfloat16),
+            pltpu.VMEM((2 * HD, tokens), jnp.bfloat16),
             pltpu.VMEM((tokens, 2 * HD), jnp.bfloat16),
             pltpu.VMEM((rows, LANES), jnp.bfloat16),
             pltpu.VMEM((SLOTS_PER_TURN * QPK * own_rows, tokens), jnp.float32),

time: 27 us -> 26 us (0.963)
  Pallas kernels: 25.5 us -> 24.4 us
    pallas_call x1, Pallas kernels: 25.5 us -> 24.4 us  [per_device(): pl.pallas_call(functools.partial(kernel, n, ng), out_shape=jax.ShapeDtype...]
where the time goes in v2:
time: 26 us; the launch traced here: 25.8 us
  Pallas kernels  24.4 us (94%)
  local copies, waits for them, and re-layouts  1.34 us (5%)
    pallas_call x1, Pallas kernels, per_device(): pl.pallas_call(functools.partial(kernel, n, ng), out_shape=jax.ShapeDtype...  24.4 us
    unnamed x1, local copies, waits for them, and re-layouts  1.34 us

profile of v2, /device:TPU:0, one launch (start us, length us, event | category | flops | bytes accessed | tf_op | source)
XLA Modules:
  0.0 25.8 jit_solution(73175213487798254)
XLA Ops:
  0.0 24.4 %shard_map.46 = bf16[4,2560]{1,0:T(4,128)(2,1)} custom-call(bf16[16,640]{1,0:T(8,128)(2,1)} %q_ref.1, bf16[4096,128]{1,0:T(8,128)(2,1)} %k_ref.1, bf16[4096,128]{1,0:T(8,128)(2,1)} %v_ref.1, s32[8,128]{1,0:T(8,128)} %bitcast.3), custom_call_target="tpu_custom_call" | custom-call | tf_op jit(solution)/shard_map/pallas_call | solution.py:197
  24.4 1.3 %copy.6 = bf16[4,2560]{1,0:T(4,128)(2,1)} copy(bf16[4,2560]{1,0:T(4,128)(2,1)} %shard_map.46) | data formatting | bytes 40960

commit v3 on v2

--- a/solution.py
+++ b/solution.py
@@ -15,7 +15,7 @@
 NEG = -1e30
 PAD = 16
 SLOTS_PER_TURN = 2
-CHUNK = 1024
+CHUNK = 256
 MESH = pl.DeviceIdType.MESH
 
 
@@ -29,7 +29,7 @@
 
 def kernel(
     n, ng, q_ref, k_ref, v_ref, b_ref, o_ref,
-    qbuf, kbuf, kext, vext, mask, score, part_out, part_in, fin_out, fin_in,
+    qbuf, kbuf, kext, vext, mask, score, rounded, part_out, part_in, fin_out, fin_in,
     local_sem, qsend, qrecv, psend, precv, fsend, frecv,
 ):
     me = lax.axis_index("ctx")
@@ -123,11 +123,10 @@
                 part = s[:, i:i + LANES]
                 top = part if top is None else jnp.maximum(top, part)
         top = jnp.max(top, axis=1, keepdims=True)
-        total = None
         for c in range(0, tokens, CHUNK):
-            w = jnp.exp((score[:, c:c + CHUNK] - top) * scale).astype(jnp.bfloat16)
-            piece = jnp.dot(w, vext[c:c + CHUNK, :], preferred_element_type=jnp.float32)
-            total = piece if total is None else total + piece
+            at = slice(c, c + CHUNK)
+            rounded[:, at] = jnp.exp((score[:, at] - top) * scale).astype(jnp.bfloat16)
+        total = jnp.dot(rounded[...], vext[...], preferred_element_type=jnp.float32)
         weight = total[:, HD:]
         part = (total[:, :HD] / weight).astype(jnp.bfloat16)
         lse = top * scale + jnp.log(weight)
@@ -206,6 +205,7 @@
             pltpu.VMEM((tokens, 2 * HD), jnp.bfloat16),
             pltpu.VMEM((rows, LANES), jnp.bfloat16),
             pltpu.VMEM((SLOTS_PER_TURN * QPK * own_rows, tokens), jnp.float32),
+            pltpu.VMEM((SLOTS_PER_TURN * QPK * own_rows, tokens), jnp.bfloat16),
             pltpu.VMEM((n, message, HD), jnp.bfloat16),
             pltpu.VMEM((n, message, HD), jnp.bfloat16),
             pltpu.VMEM((own_rows, width), jnp.bfloat16),

time: 26 us -> 26 us (level)
  no operation moved by 1% of the time
where the time goes in v3:
time: 26 us; the launch traced here: 25.8 us
  Pallas kernels  24.4 us (94%)
  local copies, waits for them, and re-layouts  1.34 us (5%)
    pallas_call x1, Pallas kernels, per_device(): pl.pallas_call(functools.partial(kernel, n, ng), out_shape=jax.ShapeDtype...  24.4 us
    unnamed x1, local copies, waits for them, and re-layouts  1.34 us

profile of v3, /device:TPU:0, one launch (start us, length us, event | category | flops | bytes accessed | tf_op | source)
XLA Modules:
  0.0 25.8 jit_solution(4099105825954124000)
XLA Ops:
  0.0 24.4 %shard_map.46 = bf16[4,2560]{1,0:T(4,128)(2,1)} custom-call(bf16[16,640]{1,0:T(8,128)(2,1)} %q_ref.1, bf16[4096,128]{1,0:T(8,128)(2,1)} %k_ref.1, bf16[4096,128]{1,0:T(8,128)(2,1)} %v_ref.1, s32[8,128]{1,0:T(8,128)} %bitcast.3), custom_call_target="tpu_custom_call" | custom-call | tf_op jit(solution)/shard_map/pallas_call | solution.py:196
  24.4 1.3 %copy.6 = bf16[4,2560]{1,0:T(4,128)(2,1)} copy(bf16[4,2560]{1,0:T(4,128)(2,1)} %shard_map.46) | data formatting | bytes 40960

commit v4 on v2

--- a/solution.py
+++ b/solution.py
@@ -29,14 +29,17 @@
 
 def kernel(
     n, ng, q_ref, k_ref, v_ref, b_ref, o_ref,
-    qbuf, kbuf, kext, vext, mask, score, part_out, part_in, fin_out, fin_in,
-    local_sem, qsend, qrecv, psend, precv, fsend, frecv,
+    qbuf, kbuf, kext, vext, mask, score, part_out, part_in,
+    local_sem, qsend, qrecv, psend, precv, ready,
 ):
     me = lax.axis_index("ctx")
     grp = lax.axis_index("grp")
     own_rows = qbuf.shape[1]
     group_rows = QPK * own_rows
     tokens = kbuf.shape[0]
+    message = part_in.shape[2]
+    out_rows = own_rows // ng
+    piece_rows = QPK * out_rows
     row_count = mask.shape[0]
     scale = 1.0 / math.sqrt(HD)
 
@@ -59,19 +62,17 @@
             device_id={"ctx": xor(me, k, n)}, device_id_type=MESH,
         )
 
-    def part_copy(k):
+    def part_copy(k, j):
+        target = xor(grp, j, ng)
         return pltpu.make_async_remote_copy(
-            src_ref=part_out.at[k], dst_ref=part_in.at[k], send_sem=psend.at[k], recv_sem=precv.at[k],
-            device_id={"ctx": xor(me, k, n)}, device_id_type=MESH,
+            src_ref=part_out.at[k, pl.ds(pl.multiple_of(target * message, PAD), message)],
+            dst_ref=part_in.at[k, j], send_sem=psend.at[k, j], recv_sem=precv.at[k, j],
+            device_id={"ctx": xor(me, k, n), "grp": target}, device_id_type=MESH,
         )
 
-    def fin_copy(j):
-        return pltpu.make_async_remote_copy(
-            src_ref=fin_out, dst_ref=fin_in.at[j], send_sem=fsend.at[j], recv_sem=frecv.at[j],
-            device_id={"grp": xor(grp, j, ng)}, device_id_type=MESH,
-        )
-
     pl.semaphore_wait(barrier, n - 1 + ng - 1)
+    for j in range(1, ng):
+        pl.semaphore_signal(ready, inc=1, device_id={"grp": xor(grp, j, ng)}, device_id_type=MESH)
     load_q.wait()
     for k in range(1, n):
         query_copy(k).start()
@@ -99,8 +100,20 @@
         at = slice(b * BLOCK, (b + 1) * BLOCK)
         kext[0:HD, at] = jnp.transpose(kbuf[at, :].astype(jnp.float32)).astype(jnp.bfloat16)
     load_v.wait()
-
-    def turn(t, carry):
+    pl.semaphore_wait(ready, ng - 1)
+
+    to_row = lax.broadcasted_iota(jnp.int32, (ng * message, group_rows + PAD), 0)
+    from_row = lax.broadcasted_iota(jnp.int32, (ng * message, group_rows + PAD), 1)
+    place = to_row % message
+    wanted = (place // out_rows) * own_rows + (to_row // message) * out_rows + place % out_rows
+    wanted = jnp.where(place < piece_rows, wanted, place - piece_rows + group_rows)
+    wanted = jnp.where(place < piece_rows + 3, wanted, -1)
+    order = jnp.where(from_row == wanted, 1.0, 0.0).astype(jnp.bfloat16)
+
+    turns = n // SLOTS_PER_TURN
+
+    def turn(step, carry):
+        t = (step + 1) % turns
         pieces = []
         for u in range(SLOTS_PER_TURN):
             k = t * SLOTS_PER_TURN + u
@@ -139,59 +152,62 @@
             mid = (line - high).astype(jnp.bfloat16).astype(jnp.float32)
             low = line - high - mid
             tail = jnp.where(pad_row == 0, high, jnp.where(pad_row == 1, mid, jnp.where(pad_row == 2, low, 0.0)))
-            part_out[k, 0:group_rows, :] = part[at]
-            part_out[k, group_rows:, :] = tail.astype(jnp.bfloat16)
+            block = jnp.concatenate([part[at], tail.astype(jnp.bfloat16)], axis=0)
+            part_out[k] = jnp.dot(order, block, preferred_element_type=jnp.float32).astype(jnp.bfloat16)
+            for j in range(1, ng):
+                part_copy(k, j).start()
 
             @pl.when(k > 0)
             def _():
-                part_copy(k).start()
+                part_copy(k, 0).start()
 
         return carry
 
-    lax.fori_loop(0, n // SLOTS_PER_TURN, turn, 0)
-
-    for k in range(1, n):
-        part_copy(k).wait_recv()
-    parts = [part_out.at[0]] + [part_in.at[k] for k in range(1, n)]
-    lines = [jnp.sum(p[group_rows:, :].astype(jnp.float32), axis=0, keepdims=True) for p in parts]
-    best = functools.reduce(jnp.maximum, lines)
-    factors = [jnp.exp(x - best) for x in lines]
-    denominator = sum(factors[1:], factors[0])
-    factors.append(jnp.zeros((LANES - n, LANES), jnp.float32))
-    columns = jnp.transpose(jnp.concatenate(factors, axis=0) / denominator)
-    result = None
-    for k, p in enumerate(parts):
-        piece = p[0:group_rows, :].astype(jnp.float32) * columns[0:group_rows, k:k + 1]
-        result = piece if result is None else result + piece
-    for h in range(QPK):
-        fin_out[:, h * HD:(h + 1) * HD] = result[h * own_rows:(h + 1) * own_rows].astype(jnp.bfloat16)
-    for j in range(1, ng):
-        fin_copy(j).start()
-
-    out_rows = own_rows // ng
+    lax.fori_loop(0, turns, turn, 0)
+
+    part_in[0, 0] = part_out[0, pl.ds(pl.multiple_of(grp * message, PAD), message), :]
     width = QPK * HD
     for j in range(ng):
-        if j > 0:
-            fin_copy(j).wait_recv()
-        whole = (fin_out if j == 0 else fin_in.at[j])[...].astype(jnp.float32)
-        mine = whole[0:out_rows]
-        for g in range(1, ng):
-            mine = jnp.where(grp == g, whole[g * out_rows:(g + 1) * out_rows], mine)
+        for k in range(n):
+            if (k, j) != (0, 0):
+                part_copy(k, j).wait_recv()
+        lines = [
+            jnp.sum(part_in[k, j, piece_rows:, :].astype(jnp.float32), axis=0, keepdims=True) for k in range(n)
+        ]
+        best = functools.reduce(jnp.maximum, lines)
+        factors = [jnp.exp(x - best) for x in lines]
+        denominator = sum(factors[1:], factors[0])
+        factors.append(jnp.zeros((LANES - n, LANES), jnp.float32))
+        columns = jnp.transpose(jnp.concatenate(factors, axis=0) / denominator)
+        picks = []
+        for h in range(QPK):
+            rows = columns[h * own_rows:(h + 1) * own_rows]
+            mine = rows[0:out_rows]
+            for g in range(1, ng):
+                mine = jnp.where(grp == g, rows[g * out_rows:(g + 1) * out_rows], mine)
+            picks.append(mine)
+        columns = jnp.concatenate(picks, axis=0)
+        result = None
+        for k in range(n):
+            piece = part_in[k, j].astype(jnp.float32)[0:piece_rows] * columns[:, k:k + 1]
+            result = piece if result is None else result + piece
         origin = xor(grp, j, ng)
-        o_ref[:, pl.ds(pl.multiple_of(origin * width, LANES), width)] = mine.astype(jnp.bfloat16)
-
-    for k in range(1, n):
-        query_copy(k).wait_send()
-        part_copy(k).wait_send()
-    for j in range(1, ng):
-        fin_copy(j).wait_send()
+        result = jnp.concatenate([result[h * out_rows:(h + 1) * out_rows] for h in range(QPK)], axis=1)
+        o_ref[:, pl.ds(pl.multiple_of(origin * width, LANES), width)] = result.astype(jnp.bfloat16)
+
+    for k in range(n):
+        if k > 0:
+            query_copy(k).wait_send()
+        for j in range(ng):
+            if (k, j) != (0, 0):
+                part_copy(k, j).wait_send()
 
 
 def per_device(n, ng, query, keys, values, blocks):
     own_rows, width = query.shape
     tokens = keys.shape[0]
     rows = blocks.shape[0]
-    message = QPK * own_rows + PAD
+    message = -(-(QPK * (own_rows // ng) + 3) // PAD) * PAD
     any_spec = pl.BlockSpec(memory_space=pl.ANY)
     vmem_spec = pl.BlockSpec(memory_space=pltpu.VMEM)
     return pl.pallas_call(
@@ -206,17 +222,14 @@
             pltpu.VMEM((tokens, 2 * HD), jnp.bfloat16),
             pltpu.VMEM((rows, LANES), jnp.bfloat16),
             pltpu.VMEM((SLOTS_PER_TURN * QPK * own_rows, tokens), jnp.float32),
-            pltpu.VMEM((n, message, HD), jnp.bfloat16),
-            pltpu.VMEM((n, message, HD), jnp.bfloat16),
-            pltpu.VMEM((own_rows, width), jnp.bfloat16),
-            pltpu.VMEM((ng, own_rows, width), jnp.bfloat16),
+            pltpu.VMEM((n, ng * message, HD), jnp.bfloat16),
+            pltpu.VMEM((n, ng, message, HD), jnp.bfloat16),
             pltpu.SemaphoreType.DMA((3,)),
             pltpu.SemaphoreType.DMA((n,)),
             pltpu.SemaphoreType.DMA((n,)),
-            pltpu.SemaphoreType.DMA((n,)),
-            pltpu.SemaphoreType.DMA((n,)),
-            pltpu.SemaphoreType.DMA((ng,)),
-            pltpu.SemaphoreType.DMA((ng,)),
+            pltpu.SemaphoreType.DMA((n, ng)),
+            pltpu.SemaphoreType.DMA((n, ng)),
+            pltpu.SemaphoreType.REGULAR,
         ],
         compiler_params=pltpu.CompilerParams(
             collective_id=0, has_side_effects=True, vmem_limit_bytes=60 * 1024 * 1024

time: 26 us -> 24.8 us (0.954)
  Pallas kernels: 24.4 us -> 23.2 us
    pallas_call x1, Pallas kernels: 24.4 us -> 23.2 us  [per_device(): pl.pallas_call(functools.partial(kernel, n, ng), out_shape=jax.ShapeDtype...]
where the time goes in v4:
time: 24.8 us; the launch traced here: 24.6 us
  Pallas kernels  23.2 us (94%)
  local copies, waits for them, and re-layouts  1.34 us (5%)
    pallas_call x1, Pallas kernels, per_device(): pl.pallas_call(functools.partial(kernel, n, ng), out_shape=jax.ShapeDtype...  23.2 us
    unnamed x1, local copies, waits for them, and re-layouts  1.34 us

profile of v4, /device:TPU:0, one launch (start us, length us, event | category | flops | bytes accessed | tf_op | source)
XLA Modules:
  0.0 24.6 jit_solution(723114708797138312)
XLA Ops:
  0.0 23.2 %shard_map.46 = bf16[4,2560]{1,0:T(4,128)(2,1)} custom-call(bf16[16,640]{1,0:T(8,128)(2,1)} %q_ref.1, bf16[4096,128]{1,0:T(8,128)(2,1)} %k_ref.1, bf16[4096,128]{1,0:T(8,128)(2,1)} %v_ref.1, s32[8,128]{1,0:T(8,128)} %bitcast.3), custom_call_target="tpu_custom_call" | custom-call | tf_op jit(solution)/shard_map/pallas_call | solution.py:213
  23.3 1.3 %copy.6 = bf16[4,2560]{1,0:T(4,128)(2,1)} copy(bf16[4,2560]{1,0:T(4,128)(2,1)} %shard_map.46) | data formatting | bytes 40960

commit v5 on v4

--- a/solution.py
+++ b/solution.py
@@ -14,7 +14,7 @@
 LANES = 128
 NEG = -1e30
 PAD = 16
-SLOTS_PER_TURN = 2
+SLOTS_PER_TURN = 4
 CHUNK = 1024
 MESH = pl.DeviceIdType.MESH
 

time: 24.8 us -> 25.6 us (1.032)
  Pallas kernels: 23.2 us -> 24.1 us
    pallas_call x1, Pallas kernels: 23.2 us -> 24.1 us  [per_device(): pl.pallas_call(functools.partial(kernel, n, ng), out_shape=jax.ShapeDtype...]
where the time goes in v5:
time: 25.6 us; the launch traced here: 25.4 us
  Pallas kernels  24.1 us (94%)
  local copies, waits for them, and re-layouts  1.34 us (5%)
    pallas_call x1, Pallas kernels, per_device(): pl.pallas_call(functools.partial(kernel, n, ng), out_shape=jax.ShapeDtype...  24.1 us
    unnamed x1, local copies, waits for them, and re-layouts  1.34 us

profile of v5, /device:TPU:0, one launch (start us, length us, event | category | flops | bytes accessed | tf_op | source)
XLA Modules:
  0.0 25.4 jit_solution(1266153637686477463)
XLA Ops:
  0.0 24.1 %shard_map.46 = bf16[4,2560]{1,0:T(4,128)(2,1)} custom-call(bf16[16,640]{1,0:T(8,128)(2,1)} %q_ref.1, bf16[4096,128]{1,0:T(8,128)(2,1)} %k_ref.1, bf16[4096,128]{1,0:T(8,128)(2,1)} %v_ref.1, s32[8,128]{1,0:T(8,128)} %bitcast.3), custom_call_target="tpu_custom_call" | custom-call | tf_op jit(solution)/shard_map/pallas_call | solution.py:213
  24.1 1.3 %copy.6 = bf16[4,2560]{1,0:T(4,128)(2,1)} copy(bf16[4,2560]{1,0:T(4,128)(2,1)} %shard_map.46) | data formatting | bytes 40960

commit v6 on v4

--- a/solution.py
+++ b/solution.py
@@ -16,24 +16,38 @@
 PAD = 16
 SLOTS_PER_TURN = 2
 CHUNK = 1024
+LOADS = 4
+UNROLL = 4
 MESH = pl.DeviceIdType.MESH
 
 
-def xor(a, b, n):
-    total, bit = 0, 1
+def bits_of(a, n):
+    bits, bit = [], 1
     while bit < n:
-        total = total + bit * ((a // bit + b // bit) % 2)
+        bits.append(lax.rem(lax.div(a, bit), 2) if not isinstance(a, int) else (a // bit) % 2)
         bit *= 2
+    return bits
+
+
+def xor(a_bits, b, n):
+    total = 0
+    for i, (x, y) in enumerate(zip(a_bits, bits_of(b, n))):
+        if isinstance(y, int):
+            total = total + (1 << i) * (1 - x if y else x)
+        else:
+            total = total + (1 << i) * (x + y - 2 * x * y)
     return total
 
 
 def kernel(
     n, ng, q_ref, k_ref, v_ref, b_ref, o_ref,
-    qbuf, kbuf, kext, vext, mask, score, part_out, part_in,
+    lists, qbuf, kbuf, kext, vext, mask, score, part_out, part_in,
     local_sem, qsend, qrecv, psend, precv, ready,
 ):
     me = lax.axis_index("ctx")
     grp = lax.axis_index("grp")
+    me_bits, grp_bits = bits_of(me, n), bits_of(grp, ng)
+    targets = [xor(grp_bits, j, ng) for j in range(ng)]
     own_rows = qbuf.shape[1]
     group_rows = QPK * own_rows
     tokens = kbuf.shape[0]
@@ -45,43 +59,65 @@
 
     barrier = pltpu.get_barrier_semaphore()
     for k in range(1, n):
-        pl.semaphore_signal(barrier, inc=1, device_id={"ctx": xor(me, k, n)}, device_id_type=MESH)
+        pl.semaphore_signal(barrier, inc=1, device_id={"ctx": xor(me_bits, k, n)}, device_id_type=MESH)
     for j in range(1, ng):
-        pl.semaphore_signal(barrier, inc=1, device_id={"grp": xor(grp, j, ng)}, device_id_type=MESH)
+        pl.semaphore_signal(barrier, inc=1, device_id={"grp": targets[j]}, device_id_type=MESH)
 
     load_q = pltpu.make_async_copy(q_ref, qbuf.at[0], local_sem.at[0])
-    load_k = pltpu.make_async_copy(k_ref, kbuf, local_sem.at[1])
-    load_v = pltpu.make_async_copy(v_ref, vext.at[:, 0:HD], local_sem.at[2])
+    load_b = pltpu.make_async_copy(b_ref, lists, local_sem.at[1])
     load_q.start()
-    load_k.start()
-    load_v.start()
+    load_b.start()
+    part_tokens = tokens // LOADS
+    load_k, load_v = [], []
+    for i in range(LOADS):
+        at = slice(i * part_tokens, (i + 1) * part_tokens)
+        load_k.append(pltpu.make_async_copy(k_ref.at[at], kbuf.at[at], local_sem.at[2 + i]))
+        load_v.append(pltpu.make_async_copy(v_ref.at[at], vext.at[at, 0:HD], local_sem.at[2 + LOADS + i]))
+    for copy in load_k + load_v:
+        copy.start()
 
     def query_copy(k):
         return pltpu.make_async_remote_copy(
             src_ref=qbuf.at[0], dst_ref=qbuf.at[k], send_sem=qsend.at[k], recv_sem=qrecv.at[k],
-            device_id={"ctx": xor(me, k, n)}, device_id_type=MESH,
+            device_id={"ctx": xor(me_bits, k, n)}, device_id_type=MESH,
         )
 
     def part_copy(k, j):
-        target = xor(grp, j, ng)
+        target = targets[j]
         return pltpu.make_async_remote_copy(
             src_ref=part_out.at[k, pl.ds(pl.multiple_of(target * message, PAD), message)],
             dst_ref=part_in.at[k, j], send_sem=psend.at[k, j], recv_sem=precv.at[k, j],
-            device_id={"ctx": xor(me, k, n), "grp": target}, device_id_type=MESH,
+            device_id={"ctx": xor(me_bits, k, n), "grp": target}, device_id_type=MESH,
         )
-
-    pl.semaphore_wait(barrier, n - 1 + ng - 1)
-    for j in range(1, ng):
-        pl.semaphore_signal(ready, inc=1, device_id={"grp": xor(grp, j, ng)}, device_id_type=MESH)
-    load_q.wait()
-    for k in range(1, n):
-        query_copy(k).start()
 
     sub = lax.broadcasted_iota(jnp.int32, (LANES, BLOCK), 0)
     for b in range(tokens // BLOCK):
         kext[HD:, b * BLOCK:(b + 1) * BLOCK] = jnp.where(sub == b, 1.0, 0.0).astype(jnp.bfloat16)
     vext[:, HD:] = jnp.ones((tokens, LANES), jnp.bfloat16)
-    listed = b_ref[...]
+    diag = (
+        lax.broadcasted_iota(jnp.int32, (group_rows, LANES), 0)
+        == lax.broadcasted_iota(jnp.int32, (group_rows, LANES), 1)
+    )
+    pad_row = lax.broadcasted_iota(jnp.int32, (PAD, LANES), 0)
+
+    to_row = lax.broadcasted_iota(jnp.int32, (ng * message, group_rows + PAD), 0)
+    from_row = lax.broadcasted_iota(jnp.int32, (ng * message, group_rows + PAD), 1)
+    message_bits, piece_bits = message.bit_length() - 1, out_rows.bit_length() - 1
+    place = to_row & (message - 1)
+    wanted = (place >> piece_bits) * own_rows + (to_row >> message_bits) * out_rows + (place & (out_rows - 1))
+    wanted = jnp.where(place < piece_rows, wanted, place - piece_rows + group_rows)
+    wanted = jnp.where(place < piece_rows + 3, wanted, -1)
+    order = jnp.where(from_row == wanted, 1.0, 0.0).astype(jnp.bfloat16)
+
+    pl.semaphore_wait(barrier, n - 1 + ng - 1)
+    for j in range(1, ng):
+        pl.semaphore_signal(ready, inc=1, device_id={"grp": targets[j]}, device_id_type=MESH)
+    load_q.wait()
+    for k in range(1, n):
+        query_copy(k).start()
+
+    load_b.wait()
+    listed = lists[...]
     block_row = lax.broadcasted_iota(jnp.int32, (tokens // BLOCK, row_count), 0)
     hit = block_row == listed[0:1, :]
     for i in range(1, listed.shape[0]):
@@ -90,39 +126,30 @@
     unused = jnp.zeros((LANES - tokens // BLOCK, row_count), jnp.float32)
     mask[...] = jnp.transpose(jnp.concatenate([bias, unused], axis=0)).astype(jnp.bfloat16)
 
-    diag = (
-        lax.broadcasted_iota(jnp.int32, (group_rows, LANES), 0)
-        == lax.broadcasted_iota(jnp.int32, (group_rows, LANES), 1)
-    )
-    pad_row = lax.broadcasted_iota(jnp.int32, (PAD, LANES), 0)
-    load_k.wait()
-    for b in range(tokens // BLOCK):
-        at = slice(b * BLOCK, (b + 1) * BLOCK)
-        kext[0:HD, at] = jnp.transpose(kbuf[at, :].astype(jnp.float32)).astype(jnp.bfloat16)
-    load_v.wait()
+    for i in range(LOADS):
+        load_k[i].wait()
+        for c in range(i * part_tokens, (i + 1) * part_tokens, BLOCK):
+            at = slice(c, c + BLOCK)
+            kext[0:HD, at] = jnp.transpose(kbuf[at, :].astype(jnp.float32)).astype(jnp.bfloat16)
+    for copy in load_v:
+        copy.wait()
     pl.semaphore_wait(ready, ng - 1)
 
-    to_row = lax.broadcasted_iota(jnp.int32, (ng * message, group_rows + PAD), 0)
-    from_row = lax.broadcasted_iota(jnp.int32, (ng * message, group_rows + PAD), 1)
-    place = to_row % message
-    wanted = (place // out_rows) * own_rows + (to_row // message) * out_rows + place % out_rows
-    wanted = jnp.where(place < piece_rows, wanted, place - piece_rows + group_rows)
-    wanted = jnp.where(place < piece_rows + 3, wanted, -1)
-    order = jnp.where(from_row == wanted, 1.0, 0.0).astype(jnp.bfloat16)
-
     turns = n // SLOTS_PER_TURN
 
     def turn(step, carry):
-        t = (step + 1) % turns
+        t = (step + 1) % turns if isinstance(step, int) else lax.rem(step + 1, turns)
         pieces = []
         for u in range(SLOTS_PER_TURN):
             k = t * SLOTS_PER_TURN + u
 
-            @pl.when(k > 0)
-            def _():
-                query_copy(k).wait_recv()
-
-            owner = xor(me, k, n)
+            if isinstance(k, int):
+                if k > 0:
+                    query_copy(k).wait_recv()
+            else:
+                pl.when(k > 0)(lambda: query_copy(k).wait_recv())
+
+            owner = xor(me_bits, k, n)
             bias = mask[pl.ds(pl.multiple_of(owner * own_rows, own_rows), own_rows), :]
             rows = qbuf[k]
             for h in range(QPK):
@@ -157,13 +184,19 @@
             for j in range(1, ng):
                 part_copy(k, j).start()
 
-            @pl.when(k > 0)
-            def _():
-                part_copy(k, 0).start()
+            if isinstance(k, int):
+                if k > 0:
+                    part_copy(k, 0).start()
+            else:
+                pl.when(k > 0)(lambda: part_copy(k, 0).start())
 
         return carry
 
-    lax.fori_loop(0, turns, turn, 0)
+    if turns <= UNROLL:
+        for step in range(turns):
+            turn(step, 0)
+    else:
+        lax.fori_loop(0, turns, turn, 0)
 
     part_in[0, 0] = part_out[0, pl.ds(pl.multiple_of(grp * message, PAD), message), :]
     width = QPK * HD
@@ -191,7 +224,7 @@
         for k in range(n):
             piece = part_in[k, j].astype(jnp.float32)[0:piece_rows] * columns[:, k:k + 1]
             result = piece if result is None else result + piece
-        origin = xor(grp, j, ng)
+        origin = targets[j]
         result = jnp.concatenate([result[h * out_rows:(h + 1) * out_rows] for h in range(QPK)], axis=1)
         o_ref[:, pl.ds(pl.multiple_of(origin * width, LANES), width)] = result.astype(jnp.bfloat16)
 
@@ -213,9 +246,10 @@
     return pl.pallas_call(
         functools.partial(kernel, n, ng),
         out_shape=jax.ShapeDtypeStruct((own_rows // ng, width * ng), jnp.bfloat16),
-        in_specs=[any_spec, any_spec, any_spec, vmem_spec],
+        in_specs=[any_spec] * 4,
         out_specs=vmem_spec,
         scratch_shapes=[
+            pltpu.VMEM((blocks.shape[2], rows), jnp.int32),
             pltpu.VMEM((n, own_rows, width), jnp.bfloat16),
             pltpu.VMEM((tokens, HD), jnp.bfloat16),
             pltpu.VMEM((2 * HD, tokens), jnp.bfloat16),
@@ -224,7 +258,7 @@
             pltpu.VMEM((SLOTS_PER_TURN * QPK * own_rows, tokens), jnp.float32),
             pltpu.VMEM((n, ng * message, HD), jnp.bfloat16),
             pltpu.VMEM((n, ng, message, HD), jnp.bfloat16),
-            pltpu.SemaphoreType.DMA((3,)),
+            pltpu.SemaphoreType.DMA((2 + 2 * LOADS,)),
             pltpu.SemaphoreType.DMA((n,)),
             pltpu.SemaphoreType.DMA((n,)),
             pltpu.SemaphoreType.DMA((n, ng)),

time: 24.8 us -> 24 us (0.968)
  Pallas kernels: 23.2 us -> 22.5 us
    pallas_call x1, Pallas kernels: 23.2 us -> 22.5 us  [per_device(): pl.pallas_call(functools.partial(kernel, n, ng), out_shape=jax.ShapeDtype...]
where the time goes in v6:
time: 24 us; the launch traced here: 23.9 us
  Pallas kernels  22.5 us (94%)
  local copies, waits for them, and re-layouts  1.34 us (6%)
    pallas_call x1, Pallas kernels, per_device(): pl.pallas_call(functools.partial(kernel, n, ng), out_shape=jax.ShapeDtype...  22.5 us
    unnamed x1, local copies, waits for them, and re-layouts  1.34 us

profile of v6, /device:TPU:0, one launch (start us, length us, event | category | flops | bytes accessed | tf_op | source)
XLA Modules:
  0.0 23.9 jit_solution(13580339337232764228)
XLA Ops:
  0.0 22.5 %shard_map.46 = bf16[4,2560]{1,0:T(4,128)(2,1)} custom-call(bf16[16,640]{1,0:T(8,128)(2,1)} %q_ref.1, bf16[4096,128]{1,0:T(8,128)(2,1)} %k_ref.1, bf16[4096,128]{1,0:T(8,128)(2,1)} %v_ref.1, s32[8,128]{1,0:T(8,128)} %bitcast.3), custom_call_target="tpu_custom_call" | custom-call | tf_op jit(solution)/shard_map/pallas_call | solution.py:246
  22.5 1.3 %copy.6 = bf16[4,2560]{1,0:T(4,128)(2,1)} copy(bf16[4,2560]{1,0:T(4,128)(2,1)} %shard_map.46) | data formatting | bytes 40960

commit v7 on v6

--- a/solution.py
+++ b/solution.py
@@ -113,7 +113,7 @@
     for j in range(1, ng):
         pl.semaphore_signal(ready, inc=1, device_id={"grp": targets[j]}, device_id_type=MESH)
     load_q.wait()
-    for k in range(1, n):
+    for k in range(n - 1, 0, -1):
         query_copy(k).start()
 
     load_b.wait()
@@ -138,7 +138,7 @@
     turns = n // SLOTS_PER_TURN
 
     def turn(step, carry):
-        t = (step + 1) % turns if isinstance(step, int) else lax.rem(step + 1, turns)
+        t = turns - 1 - step
         pieces = []
         for u in range(SLOTS_PER_TURN):
             k = t * SLOTS_PER_TURN + u

time: 24 us -> 23.8 us (level)
  no operation moved by 1% of the time
where the time goes in v7:
time: 23.8 us; the launch traced here: 23.7 us
  Pallas kernels  22.3 us (94%)
  local copies, waits for them, and re-layouts  1.34 us (6%)
    pallas_call x1, Pallas kernels, per_device(): pl.pallas_call(functools.partial(kernel, n, ng), out_shape=jax.ShapeDtype...  22.3 us
    unnamed x1, local copies, waits for them, and re-layouts  1.34 us

profile of v7, /device:TPU:0, one launch (start us, length us, event | category | flops | bytes accessed | tf_op | source)
XLA Modules:
  0.0 23.7 jit_solution(1885726093984755539)
XLA Ops:
  0.0 22.3 %shard_map.46 = bf16[4,2560]{1,0:T(4,128)(2,1)} custom-call(bf16[16,640]{1,0:T(8,128)(2,1)} %q_ref.1, bf16[4096,128]{1,0:T(8,128)(2,1)} %k_ref.1, bf16[4096,128]{1,0:T(8,128)(2,1)} %v_ref.1, s32[8,128]{1,0:T(8,128)} %bitcast.3), custom_call_target="tpu_custom_call" | custom-call | tf_op jit(solution)/shard_map/pallas_call | solution.py:246
  22.3 1.3 %copy.6 = bf16[4,2560]{1,0:T(4,128)(2,1)} copy(bf16[4,2560]{1,0:T(4,128)(2,1)} %shard_map.46) | data formatting | bytes 40960

commit v8 on v7

--- a/solution.py
+++ b/solution.py
@@ -56,6 +56,7 @@
     piece_rows = QPK * out_rows
     row_count = mask.shape[0]
     scale = 1.0 / math.sqrt(HD)
+    log2_scale = scale * math.log2(math.e)
 
     barrier = pltpu.get_barrier_semaphore()
     for k in range(1, n):
@@ -165,7 +166,7 @@
         top = jnp.max(top, axis=1, keepdims=True)
         total = None
         for c in range(0, tokens, CHUNK):
-            w = jnp.exp((score[:, c:c + CHUNK] - top) * scale).astype(jnp.bfloat16)
+            w = jnp.exp2(((score[:, c:c + CHUNK] - top) * log2_scale).astype(jnp.bfloat16))
             piece = jnp.dot(w, vext[c:c + CHUNK, :], preferred_element_type=jnp.float32)
             total = piece if total is None else total + piece
         weight = total[:, HD:]

time: 23.8 us -> 23.8 us (level)
  no operation moved by 1% of the time
where the time goes in v8:
time: 23.8 us; the launch traced here: 23.6 us
  Pallas kernels  22.2 us (93%)
  local copies, waits for them, and re-layouts  1.34 us (6%)
    pallas_call x1, Pallas kernels, per_device(): pl.pallas_call(functools.partial(kernel, n, ng), out_shape=jax.ShapeDtype...  22.2 us
    unnamed x1, local copies, waits for them, and re-layouts  1.34 us

profile of v8, /device:TPU:0, one launch (start us, length us, event | category | flops | bytes accessed | tf_op | source)
XLA Modules:
  0.0 23.6 jit_solution(3969338298595923820)
XLA Ops:
  0.0 22.2 %shard_map.46 = bf16[4,2560]{1,0:T(4,128)(2,1)} custom-call(bf16[16,640]{1,0:T(8,128)(2,1)} %q_ref.1, bf16[4096,128]{1,0:T(8,128)(2,1)} %k_ref.1, bf16[4096,128]{1,0:T(8,128)(2,1)} %v_ref.1, s32[8,128]{1,0:T(8,128)} %bitcast.3), custom_call_target="tpu_custom_call" | custom-call | tf_op jit(solution)/shard_map/pallas_call | solution.py:247
  22.3 1.3 %copy.6 = bf16[4,2560]{1,0:T(4,128)(2,1)} copy(bf16[4,2560]{1,0:T(4,128)(2,1)} %shard_map.46) | data formatting | bytes 40960

commit v9 on v7

--- a/solution.py
+++ b/solution.py
@@ -40,8 +40,8 @@
 
 
 def kernel(
-    n, ng, q_ref, k_ref, v_ref, b_ref, o_ref,
-    lists, qbuf, kbuf, kext, vext, mask, score, part_out, part_in,
+    n, ng, q_ref, k_ref, v_ref, b_ref, part_in,
+    lists, qbuf, kbuf, kext, vext, mask, score, part_out,
     local_sem, qsend, qrecv, psend, precv, ready,
 ):
     me = lax.axis_index("ctx")
@@ -78,7 +78,7 @@
 
     def query_copy(k):
         return pltpu.make_async_remote_copy(
-            src_ref=qbuf.at[0], dst_ref=qbuf.at[k], send_sem=qsend.at[k], recv_sem=qrecv.at[k],
+            src_ref=qbuf.at[0], dst_ref=qbuf.at[k], send_sem=qsend, recv_sem=qrecv.at[k],
             device_id={"ctx": xor(me_bits, k, n)}, device_id_type=MESH,
         )
 
@@ -86,8 +86,13 @@
         target = targets[j]
         return pltpu.make_async_remote_copy(
             src_ref=part_out.at[k, pl.ds(pl.multiple_of(target * message, PAD), message)],
-            dst_ref=part_in.at[k, j], send_sem=psend.at[k, j], recv_sem=precv.at[k, j],
+            dst_ref=part_in.at[k, j], send_sem=psend.at[0 if isinstance(k, int) and k == 0 else 1], recv_sem=precv,
             device_id={"ctx": xor(me_bits, k, n), "grp": target}, device_id_type=MESH,
+        )
+
+    def part_keep():
+        return pltpu.make_async_copy(
+            part_out.at[0, pl.ds(pl.multiple_of(grp * message, PAD), message)], part_in.at[0, 0], precv
         )
 
     sub = lax.broadcasted_iota(jnp.int32, (LANES, BLOCK), 0)
@@ -183,12 +188,10 @@
             part_out[k] = jnp.dot(order, block, preferred_element_type=jnp.float32).astype(jnp.bfloat16)
             for j in range(1, ng):
                 part_copy(k, j).start()
-
-            if isinstance(k, int):
-                if k > 0:
-                    part_copy(k, 0).start()
+            if isinstance(k, int) and k == 0:
+                part_keep().start()
             else:
-                pl.when(k > 0)(lambda: part_copy(k, 0).start())
+                part_copy(k, 0).start()
 
         return carry
 
@@ -196,14 +199,23 @@
         for step in range(turns):
             turn(step, 0)
     else:
-        lax.fori_loop(0, turns, turn, 0)
-
-    part_in[0, 0] = part_out[0, pl.ds(pl.multiple_of(grp * message, PAD), message), :]
+        lax.fori_loop(0, turns - 1, turn, 0)
+        turn(turns - 1, 0)
+
+    for finished, semaphore in (
+        (part_in, precv), (part_out.at[0, pl.ds(0, (ng - 1) * message)], psend.at[0]),
+        (part_out.at[pl.ds(1, n - 1)], psend.at[1]), (qbuf.at[pl.ds(1, n - 1)], qsend),
+    ):
+        pltpu.make_async_copy(finished, finished, semaphore).wait()
+
+
+def combine(n, ng, own_rows, part_in, o_ref):
+    grp = lax.axis_index("grp")
+    grp_bits = bits_of(grp, ng)
+    out_rows = own_rows // ng
+    piece_rows = QPK * out_rows
     width = QPK * HD
     for j in range(ng):
-        for k in range(n):
-            if (k, j) != (0, 0):
-                part_copy(k, j).wait_recv()
         lines = [
             jnp.sum(part_in[k, j, piece_rows:, :].astype(jnp.float32), axis=0, keepdims=True) for k in range(n)
         ]
@@ -224,16 +236,9 @@
         for k in range(n):
             piece = part_in[k, j].astype(jnp.float32)[0:piece_rows] * columns[:, k:k + 1]
             result = piece if result is None else result + piece
-        origin = targets[j]
+        origin = xor(grp_bits, j, ng)
         result = jnp.concatenate([result[h * out_rows:(h + 1) * out_rows] for h in range(QPK)], axis=1)
         o_ref[:, pl.ds(pl.multiple_of(origin * width, LANES), width)] = result.astype(jnp.bfloat16)
-
-    for k in range(n):
-        if k > 0:
-            query_copy(k).wait_send()
-        for j in range(ng):
-            if (k, j) != (0, 0):
-                part_copy(k, j).wait_send()
 
 
 def per_device(n, ng, query, keys, values, blocks):
@@ -243,11 +248,11 @@
     message = -(-(QPK * (own_rows // ng) + 3) // PAD) * PAD
     any_spec = pl.BlockSpec(memory_space=pl.ANY)
     vmem_spec = pl.BlockSpec(memory_space=pltpu.VMEM)
-    return pl.pallas_call(
+    parts = pl.pallas_call(
         functools.partial(kernel, n, ng),
-        out_shape=jax.ShapeDtypeStruct((own_rows // ng, width * ng), jnp.bfloat16),
+        out_shape=jax.ShapeDtypeStruct((n, ng, message, HD), jnp.bfloat16),
         in_specs=[any_spec] * 4,
-        out_specs=vmem_spec,
+        out_specs=any_spec,
         scratch_shapes=[
             pltpu.VMEM((blocks.shape[2], rows), jnp.int32),
             pltpu.VMEM((n, own_rows, width), jnp.bfloat16),
@@ -257,18 +262,23 @@
             pltpu.VMEM((rows, LANES), jnp.bfloat16),
             pltpu.VMEM((SLOTS_PER_TURN * QPK * own_rows, tokens), jnp.float32),
             pltpu.VMEM((n, ng * message, HD), jnp.bfloat16),
-            pltpu.VMEM((n, ng, message, HD), jnp.bfloat16),
             pltpu.SemaphoreType.DMA((2 + 2 * LOADS,)),
+            pltpu.SemaphoreType.DMA,
             pltpu.SemaphoreType.DMA((n,)),
-            pltpu.SemaphoreType.DMA((n,)),
-            pltpu.SemaphoreType.DMA((n, ng)),
-            pltpu.SemaphoreType.DMA((n, ng)),
+            pltpu.SemaphoreType.DMA((2,)),
+            pltpu.SemaphoreType.DMA,
             pltpu.SemaphoreType.REGULAR,
         ],
         compiler_params=pltpu.CompilerParams(
             collective_id=0, has_side_effects=True, vmem_limit_bytes=60 * 1024 * 1024
         ),
     )(query, keys, values, jnp.transpose(blocks, (1, 2, 0))[0])
+    return pl.pallas_call(
+        functools.partial(combine, n, ng, own_rows),
+        out_shape=jax.ShapeDtypeStruct((own_rows // ng, width * ng), jnp.bfloat16),
+        in_specs=[vmem_spec],
+        out_specs=vmem_spec,
+    )(parts)
 
 
 def solution(mesh):

time: 23.8 us -> 22.5 us (0.945)
  local copies, waits for them, and re-layouts: 1.34 us -> 0 us
    pallas_call x0 -> x1, Pallas kernels: none -> 1.9 us  [per_device(): pl.pallas_call(functools.partial(combine, n, ng, own_rows), out_shape=jax...]
    pallas_call x1, Pallas kernels: 22.3 us -> 20.5 us  [per_device(): pl.pallas_call(functools.partial(kernel, n, ng), out_shape=jax.ShapeDtype...]
    unnamed x1 -> x0, local copies, waits for them, and re-layouts: 1.34 us -> none
where the time goes in v9:
time: 22.5 us; the launch traced here: 22.4 us
  Pallas kernels  22.4 us (100%)
    pallas_call x1, Pallas kernels, per_device(): pl.pallas_call(functools.partial(kernel, n, ng), out_shape=jax.ShapeDtype...  20.5 us
    pallas_call x1, Pallas kernels, per_device(): pl.pallas_call(functools.partial(combine, n, ng, own_rows), out_shape=jax...  1.9 us

profile of v9, /device:TPU:0, one launch (start us, length us, event | category | flops | bytes accessed | tf_op | source)
XLA Modules:
  0.0 22.4 jit_solution(11806471869284942995)
XLA Ops:
  0.0 20.5 %shard_map.46.part_in = bf16[8,4,32,128]{3,2,1,0:T(8,128)(2,1)} custom-call(bf16[16,640]{1,0:T(8,128)(2,1)} %q_ref.1, bf16[4096,128]{1,0:T(8,128)(2,1)} %k_ref.1, bf16[4096,128]{1,0:T(8,128)(2,1)} %v_ref.1, s32[8,128]{1,0:T(8,128)} %bitcast.3), custom_call_target="tpu_custom_call" | custom-call | tf_op jit(solution)/shard_map/pallas_call | solution.py:251
  20.5 1.9 %shard_map.47 = bf16[4,2560]{1,0:T(4,128)(2,1)} custom-call(bf16[8,4,32,128]{3,2,1,0:T(8,128)(2,1)} %shard_map.46.part_in), custom_call_target="tpu_custom_call" | custom-call | tf_op jit(solution)/shard_map/pallas_call | solution.py:276

commit v10 on v9

--- a/solution.py
+++ b/solution.py
@@ -142,8 +142,7 @@
 
     turns = n // SLOTS_PER_TURN
 
-    def turn(step, carry):
-        t = turns - 1 - step
+    def prepare(t):
         pieces = []
         for u in range(SLOTS_PER_TURN):
             k = t * SLOTS_PER_TURN + u
@@ -160,19 +159,22 @@
             for h in range(QPK):
                 pieces.append(jnp.concatenate([rows[:, h * HD:(h + 1) * HD], bias], axis=1))
         query = jnp.concatenate(pieces, axis=0)
-        top = None
-        for c in range(0, tokens, CHUNK):
-            s = jnp.dot(query, kext[:, c:c + CHUNK], preferred_element_type=jnp.float32)
-            score[:, c:c + CHUNK] = s
-            for i in range(0, CHUNK, LANES):
-                part = s[:, i:i + LANES]
-                top = part if top is None else jnp.maximum(top, part)
-        top = jnp.max(top, axis=1, keepdims=True)
-        total = None
-        for c in range(0, tokens, CHUNK):
-            w = jnp.exp((score[:, c:c + CHUNK] - top) * scale).astype(jnp.bfloat16)
-            piece = jnp.dot(w, vext[c:c + CHUNK, :], preferred_element_type=jnp.float32)
-            total = piece if total is None else total + piece
+        return query
+
+    def scores(query, buffer, c, top):
+        s = jnp.dot(query, kext[:, c:c + CHUNK], preferred_element_type=jnp.float32)
+        score[buffer, :, c:c + CHUNK] = s
+        for i in range(0, CHUNK, LANES):
+            part = s[:, i:i + LANES]
+            top = part if top is None else jnp.maximum(top, part)
+        return top
+
+    def attend(buffer, c, top, total):
+        w = jnp.exp((score[buffer, :, c:c + CHUNK] - top) * scale).astype(jnp.bfloat16)
+        piece = jnp.dot(w, vext[c:c + CHUNK, :], preferred_element_type=jnp.float32)
+        return piece if total is None else total + piece
+
+    def finish(t, top, total):
         weight = total[:, HD:]
         part = (total[:, :HD] / weight).astype(jnp.bfloat16)
         lse = top * scale + jnp.log(weight)
@@ -193,11 +195,33 @@
             else:
                 part_copy(k, 0).start()
 
+    def turn(step, carry):
+        t = turns - 1 - step
+        query = prepare(t)
+        top, total = None, None
+        for c in range(0, tokens, CHUNK):
+            top = scores(query, 0, c, top)
+        top = jnp.max(top, axis=1, keepdims=True)
+        for c in range(0, tokens, CHUNK):
+            total = attend(0, c, top, total)
+        finish(t, top, total)
         return carry
 
     if turns <= UNROLL:
+        query, top = prepare(turns - 1), None
+        for c in range(0, tokens, CHUNK):
+            top = scores(query, 0, c, top)
         for step in range(turns):
-            turn(step, 0)
+            t = turns - 1 - step
+            now, total, later = jnp.max(top, axis=1, keepdims=True), None, None
+            if t > 0:
+                query = prepare(t - 1)
+            for c in range(0, tokens, CHUNK):
+                if t > 0:
+                    later = scores(query, (step + 1) % 2, c, later)
+                total = attend(step % 2, c, now, total)
+            finish(t, now, total)
+            top = later
     else:
         lax.fori_loop(0, turns - 1, turn, 0)
         turn(turns - 1, 0)
@@ -260,7 +284,7 @@
             pltpu.VMEM((2 * HD, tokens), jnp.bfloat16),
             pltpu.VMEM((tokens, 2 * HD), jnp.bfloat16),
             pltpu.VMEM((rows, LANES), jnp.bfloat16),
-            pltpu.VMEM((SLOTS_PER_TURN * QPK * own_rows, tokens), jnp.float32),
+            pltpu.VMEM((2, SLOTS_PER_TURN * QPK * own_rows, tokens), jnp.float32),
             pltpu.VMEM((n, ng * message, HD), jnp.bfloat16),
             pltpu.SemaphoreType.DMA((2 + 2 * LOADS,)),
             pltpu.SemaphoreType.DMA,

time: 22.5 us -> 22.1 us (0.982)
  Pallas kernels: 22.4 us -> 21.9 us
    pallas_call x1, Pallas kernels: 20.5 us -> 20 us  [per_device(): pl.pallas_call(functools.partial(kernel, n, ng), out_shape=jax.ShapeDtype...]
where the time goes in v10:
time: 22.1 us; the launch traced here: 21.9 us
  Pallas kernels  21.9 us (99%)
    pallas_call x1, Pallas kernels, per_device(): pl.pallas_call(functools.partial(kernel, n, ng), out_shape=jax.ShapeDtype...  20 us
    pallas_call x1, Pallas kernels, per_device(): pl.pallas_call(functools.partial(combine, n, ng, own_rows), out_shape=jax...  1.9 us

profile of v10, /device:TPU:0, one launch (start us, length us, event | category | flops | bytes accessed | tf_op | source)
XLA Modules:
  0.0 21.9 jit_solution(14510799152026538808)
XLA Ops:
  0.0 20.0 %shard_map.46.part_in = bf16[8,4,32,128]{3,2,1,0:T(8,128)(2,1)} custom-call(bf16[16,640]{1,0:T(8,128)(2,1)} %q_ref.1, bf16[4096,128]{1,0:T(8,128)(2,1)} %k_ref.1, bf16[4096,128]{1,0:T(8,128)(2,1)} %v_ref.1, s32[8,128]{1,0:T(8,128)} %bitcast.3), custom_call_target="tpu_custom_call" | custom-call | tf_op jit(solution)/shard_map/pallas_call | solution.py:275
  20.0 1.9 %shard_map.47 = bf16[4,2560]{1,0:T(4,128)(2,1)} custom-call(bf16[8,4,32,128]{3,2,1,0:T(8,128)(2,1)} %shard_map.46.part_in), custom_call_target="tpu_custom_call" | custom-call | tf_op jit(solution)/shard_map/pallas_call | solution.py:300
